TPU v7x, 256 devices: a whole 4x4x8 slice. The times are simulated.
256 devices in a mesh: cuts: 4 (over y_lo, core), shard: 64 (over z, x, y_hi).
Axes of the slice: x: 4, y: 4 (y_hi: 2, y_lo: 2; y = y_hi * 2 + y_lo), z: 8, core: 2. Of those that a mesh axis runs over, the one named last changes fastest.
Arguments:
- stems: float32 [4, 2, 16384, 8, 256], P('cuts', None, 'shard'), may hold values from -6 to 6
- slice_branches: float32 [6, 3, 2, 256, 256], replicated, may hold values from -0.25 to 0.25
- closing: float32 [2, 256, 256], replicated, may hold values from -0.25 to 0.25
- path: int32 [3], replicated, may hold values from 0 to 2, each once
- slice_assign: int32 [6], replicated, may hold values from 0 to 5, each once
Outputs:
- amplitudes: float32 [2, 16384, 8, 256], P(None, 'shard', 'cuts')
Inputs may be any that keep to these rules, and one draw needn't show every extreme that they name: `path`: each value appears once. `slice_assign`: each value appears once.
All inputs are finite; a program needn't handle non-finite values.
Results may differ from a plain program's by a relative error of at most 0.00012.
Values sent between devices are 32-bit elements; how exact they have to be, the bound alone decides.
No kernel may reach another device: no remote copies, remote signals or barrier semaphores. Data moves between devices by JAX's collectives and lax.ppermute only.
A program may use at most 128 MiB of HBM per device.

v0:
```python
import jax
import jax.numpy as jnp
from jax import lax
from jax.sharding import PartitionSpec as P

HIGH = lax.Precision.HIGHEST


def right_apply(field, matrix):
    prod = jnp.einsum("plmk,qkn->pqlmn", field, matrix, precision=HIGH)
    return jnp.stack([prod[0, 0] - prod[1, 1], prod[0, 1] + prod[1, 0]])


def left_apply(field, matrix):
    prod = jnp.einsum("plmk,qln->pqnmk", field, matrix, precision=HIGH)
    return jnp.stack([prod[0, 0] - prod[1, 1], prod[0, 1] + prod[1, 0]])


def per_device(stems, slice_branches, closing, path, slice_assign):
    slot_value = lax.dynamic_index_in_dim(slice_assign, lax.axis_index("cuts"), 0, keepdims=False)
    mine = lax.dynamic_index_in_dim(slice_branches, slot_value, 0, keepdims=False)

    def branch_at(step):
        return lax.dynamic_index_in_dim(mine, path[step], 0, keepdims=False)

    field = stems[0]
    field = left_apply(field, branch_at(0))
    field = right_apply(field, branch_at(1))
    field = left_apply(
        lax.all_to_all(field, "shard", split_axis=1, concat_axis=1, tiled=True), branch_at(2)
    )
    field = right_apply(
        lax.all_to_all(field, "shard", split_axis=3, concat_axis=3, tiled=True), closing
    )
    return lax.psum_scatter(field, "cuts", scatter_dimension=2, tiled=True)


def solution(mesh):
    return jax.shard_map(
        per_device,
        mesh=mesh,
        in_specs=(P("cuts", None, "shard", None, None), P(), P(), P(), P()),
        out_specs=P(None, "shard", "cuts", None),
        check_vma=False,
    )
```

profile of v0, /device:TPU:1, one launch (start us, length us, event | category | flops | bytes accessed | tf_op | source)
XLA Modules:
  0.0 400.8 jit_solution(1105642642306605271)
XLA Ops:
  6.5 0.0 copy-start
  6.5 1.3 dynamic_slice.16
  9.1 1.4 fusion.44
  12.9 10.7 %fusion.11 = f32[2,2,256,8,256]{4,2,3,0,1:T(8,128)S(1)} fusion(f32[2,256,8,256]{3,2,1,0:T(8,128)} %bitcast.124, f32[6,3,2,256,256]{4,3,2,1,0:T(8,128)} %param.6, s32[]{:T(128)S(6)} %select_n.28, s32[]{:T(128)S(6)} %select_n.34), kind=kOutput, calls=%fused_computation.15 | convolution fusion | flops 6442450944 | bytes 13107208 | tf_op jit(solution)/shard_map/plmk,qln->pqnmk/dot_general | solution.py:15
  23.6 0.3 fusion.30
  23.9 1.6 fusion.32
  27.2 16.2 %fusion.20 = f32[2,2,256,8,256]{2,4,3,0,1:T(8,128)S(1)} fusion(f32[1,256,8,256]{3,1,2,0:T(8,128)S(1)} %fusion.30, f32[1,256,8,256]{3,1,2,0:T(8,128)} %fusion.32, f32[6,3,2,256,256]{4,3,2,1,0:T(8,128)} %param.6, s32[]{:T(128)S(6)} %select_n.28, s32[]{:T(128)S(6)} %select_n.32), kind=kOutput, calls=%fused_computation.18 | convolution fusion | flops 6443499520 | bytes 13107208 | tf_op jit(solution)/shard_map/plmk,qkn->pqlmn/dot_general | solution.py:10
  43.3 0.3 fusion.27
  43.6 0.3 fusion.29
  43.9 2.2 pad_maximum_fusion
  46.1 5.5 %copy.28 = f32[2,256,8,256]{3,2,0,1:T(8,128)} copy(f32[2,256,8,256]{1,3,2,0:T(8,128)} %pad_maximum_fusion) | data formatting | bytes 8388608 | tf_op jit(solution)/shard_map/stack | solution.py:11
  51.6 15.4 %all-to-all-start = ((f32[2,256,8,256]{3,2,0,1:T(8,128)}), f32[2,256,8,256]{3,2,0,1:T(8,128)}, u32[]{:S(2)}, u32[]{:S(2)}) async-start(f32[2,256,8,256]{3,2,0,1:T(8,128)} %copy.28), calls=%async_computation | async-start | bytes 8388608 | tf_op jit(solution)/shard_map/all_to_all | solution.py:30
  67.0 0.0 all-reduce.3.cloned.1.call-start
  68.9 90.6 %all-to-all-done = f32[2,256,8,256]{3,2,0,1:T(8,128)} async-done(((f32[2,256,8,256]{3,2,0,1:T(8,128)}), f32[2,256,8,256]{3,2,0,1:T(8,128)}, u32[]{:S(2)}, u32[]{:S(2)}) %all-to-all-start) | async-done | bytes 4194336 | tf_op jit(solution)/shard_map/all_to_all | solution.py:30
  159.5 10.9 %fusion.14 = f32[2,2,256,8,256]{4,2,3,0,1:T(8,128)S(1)} fusion(f32[2,256,8,256]{3,2,0,1:T(8,128)} %all-to-all-done, f32[6,3,2,256,256]{4,3,2,1,0:T(8,128)} %param.6, s32[]{:T(128)S(6)} %select_n.28, s32[]{:T(128)S(6)} %select_n.30), kind=kOutput, calls=%fused_computation.16 | convolution fusion | flops 6442450944 | bytes 13107208 | tf_op jit(solution)/shard_map/plmk,qln->pqnmk/dot_general | solution.py:15
  170.4 0.3 fusion.24
  170.7 0.3 fusion.26
  171.0 2.2 pad_maximum_fusion.1
  173.2 5.5 %copy.32 = f32[2,256,8,256]{1,2,0,3:T(8,128)} copy(f32[2,256,8,256]{3,1,2,0:T(8,128)} %pad_maximum_fusion.1) | data formatting | bytes 8388608 | tf_op jit(solution)/shard_map/stack | solution.py:16
  178.7 102.1 %all_to_all.10 = f32[2,256,8,256]{1,2,0,3:T(8,128)S(1)} all-to-all(f32[2,256,8,256]{1,2,0,3:T(8,128)} %copy.32), channel_id=1, replica_groups=mesh['cuts'=4,'shard'=64] {'shard'}, dimensions={3} | all-to-all | bytes 8388608 | tf_op jit(solution)/shard_map/all_to_all | solution.py:33
  280.8 0.0 copy-done
  280.8 10.1 %fusion.17 = f32[2,2,256,8,256]{4,2,1,3,0:T(8,128)S(1)} fusion(f32[2,256,8,256,1]{1,2,0,3,4:T(8,128)S(1)} %bitcast.123, f32[2,256,256]{2,1,0:T(8,128)S(1)} %copy-done), kind=kOutput, calls=%fused_computation.17 | convolution fusion | flops 6442450944 | bytes 13107200 | tf_op jit(solution)/shard_map/plmk,qkn->pqlmn/dot_general | solution.py:10
  290.9 0.3 fusion.21
  291.2 0.3 fusion.23
  291.5 2.2 pad_maximum_fusion.2
  293.7 0.0 copy-start.1
  293.7 0.0 all-reduce.3.cloned.1.call-update
  293.7 0.6 copy-done.1
  294.4 0.6 dynamic-slice.6
  295.6 95.0 %all-reduce.3.cloned.1.call-done = f32[2,256,8,256]{3,1,2,0:T(8,128)} async-done(((f32[2,256,8,256]{3,1,2,0:T(8,128)}), f32[2,256,8,256]{3,1,2,0:T(8,128)}) %all-reduce.3.cloned.1.call-update) | async-done | bytes 4194320
  390.6 1.3 constant_dynamic-slice_fusion
  391.9 1.8 copy.36
Async XLA Ops:
  6.5 274.3 %copy-start = (f32[2,256,256]{2,1,0:T(8,128)S(1)}, f32[2,256,256]{2,1,0:T(8,128)}, u32[]{:S(2)}) copy-start(f32[2,256,256]{2,1,0:T(8,128)} %param.7) | copy-start | bytes 1572868
  51.6 107.9 %all-to-all-start = ((f32[2,256,8,256]{3,2,0,1:T(8,128)}), f32[2,256,8,256]{3,2,0,1:T(8,128)}, u32[]{:S(2)}, u32[]{:S(2)}) async-start(f32[2,256,8,256]{3,2,0,1:T(8,128)} %copy.28), calls=%async_computation | async-start | bytes 8388608 | tf_op jit(solution)/shard_map/all_to_all | solution.py:30
  67.0 323.6 %all-reduce.3.cloned.1.call-start = ((), (), s32[]{:S(2)}) async-start(), calls=%async_computation.2 | async-start | bytes 8388608
  293.7 0.7 copy-start.1
Sparse Core Ops, SparseCore 0:
  293.9 96.7 all-reduce.2
where the time goes:
time: 405 us; the launch traced here: 401 us
  waiting for transfers between devices  186 us (46%)
  blocking collectives  102 us (25%)
  matrix products  47.8 us (12%)
  between operations  21.6 us (5%)
  local copies, waits for them, and re-layouts  18 us (4%)
  starting transfers between devices  15.4 us (4%)
  other arithmetic  10.2 us (3%)
    all_to_all x1, blocking collectives, per_device(): lax.all_to_all(field, 'shard', split_axis=3, concat_axis=3, tiled=True)  102 us
    unnamed x2, waiting for transfers between devices  95 us
    all_to_all x1, waiting for transfers between devices, per_device(): lax.all_to_all(field, 'shard', split_axis=1, concat_axis=1, tiled=True)  90.6 us
    dot_general x2, matrix products, right_apply(): prod = jnp.einsum('plmk,qkn->pqlmn', field, matrix, precision=HIGH)  26.3 us
    dot_general x2, matrix products, left_apply(): prod = jnp.einsum('plmk,qln->pqnmk', field, matrix, precision=HIGH)  21.6 us
    all_to_all x1, starting transfers between devices, per_device(): lax.all_to_all(field, 'shard', split_axis=1, concat_axis=1, tiled=True)  15.4 us
  transfers between devices with their start and end apart: 2, of which 2 were waited for; matrix products, arithmetic and copies ran while one was open for 0% of the time, Pallas kernels for 0%

commit v1 on v0

v1 whole, which is shorter than its diff:
```python
import functools

import jax
import jax.numpy as jnp
from jax import lax
from jax.experimental import pallas as pl
from jax.experimental.pallas import tpu as pltpu
from jax.sharding import PartitionSpec as P

BF, F32 = jnp.bfloat16, jnp.float32
ALL = ("cuts", "shard")
NN = (((1,), (0,)), ((), ()))
NT = (((1,), (1,)), ((), ()))


def halves(x):
    high = x.astype(BF)
    return high, (x - high.astype(F32)).astype(BF)


def dot3(left, right, dims):
    dot = functools.partial(lax.dot_general, dimension_numbers=dims, preferred_element_type=F32)
    return dot(left[0], right[0]) + (dot(left[0], right[1]) + dot(left[1], right[0]))


def put(pair, rows, cols, value):
    high, low = halves(value)
    pair[0, rows, cols] = high
    pair[1, rows, cols] = low


def complex_blocks(pair, part, rows, cols, value):
    up = pl.ds(rows.start, rows.size), pl.ds(256 + rows.start, rows.size)
    across = pl.ds(cols.start, cols.size), pl.ds(256 + cols.start, cols.size)
    if part == 0:
        put(pair, up[0], across[0], value)
        put(pair, up[1], across[1], value)
    else:
        put(pair, up[1], across[0], value)
        put(pair, up[0], across[1], -value)


def before_kernel(assign, path, branches, x0, x1, send, v, tmp, a0, a1, sem):
    m = pl.program_id(0)

    @pl.when(m == 0)
    def _():
        value = assign[lax.axis_index("cuts")]
        copies = [pltpu.make_async_copy(branches.at[value, path[i]], v.at[i], sem.at[i]) for i in range(2)]
        for copy in copies:
            copy.start()
        for i, pair in enumerate((a0, a1)):
            copies[i].wait()
            for part in range(2):
                turned = v[i, part].T
                for half in range(2):
                    tmp[half] = turned[:, 128 * half : 128 * half + 128]
                for half in range(2):
                    for b in range(4):
                        value = tmp[half, pl.ds(b, 64, stride=4), :]
                        complex_blocks(pair, part, pl.ds(64 * b, 64), pl.ds(128 * half, 128), value)

    x = jnp.concatenate(
        [
            jnp.concatenate([x0[p, pl.ds(m, 256, stride=8), :], x1[p, pl.ds(m, 256, stride=8), :]], axis=1)
            for p in range(2)
        ],
        axis=0,
    )
    z = dot3((a0[0], a0[1]), halves(x), NN)
    z = jnp.concatenate([z[:256], z[256:]], axis=1)
    y = dot3((a1[0], a1[1]), halves(z), NT)
    low_lane = lax.broadcasted_iota(jnp.int32, (64, 128), 1) < 64
    for q in range(2):
        for bph in range(2):
            for bh in range(2):
                row = 256 * q + 128 * bph
                one = y[row : row + 64, 128 * bh : 128 * bh + 128]
                two = y[row + 64 : row + 128, 128 * bh : 128 * bh + 128]
                one_turned, two_turned = pltpu.roll(one, 64, 1), pltpu.roll(two, 64, 1)
                r = 16 * (m % 2) + ((q * 2 + bph) * 4 + bh * 2)
                send[pl.ds(r, 64, stride=32), :] = jnp.where(low_lane, one, two_turned)
                send[pl.ds(r + 1, 64, stride=32), :] = jnp.where(low_lane, one_turned, two)


def after_kernel(assign, path, branches, closing, got, out, v, c, tmp, a2, c2, total, sem):
    s = pl.program_id(0)

    def fetch(i):
        return pltpu.make_async_copy(branches.at[assign[i], path[2]], v.at[lax.rem(i, 2)], sem.at[lax.rem(i, 2)])

    @pl.when(s == 0)
    def _():
        fetch(0).start()
        pltpu.make_async_copy(closing, c, sem.at[2]).start()

    @pl.when(s < 3)
    def _():
        fetch(s + 1).start()

    fetch(s).wait()
    for part in range(2):
        for half in range(2):
            tmp[half] = v[lax.rem(s, 2), part, :, pl.ds(128 * half, 128)]
        for half in range(2):
            moved = jnp.concatenate([tmp[half, pl.ds(b, 64, stride=4), :] for b in range(4)], axis=0)
            complex_blocks(a2, part, pl.ds(128 * half, 128), pl.ds(0, 256), moved.T)

    def rows_of(mj, p, bph):
        return jnp.concatenate(
            [got[pl.ds(((mj * 2 + p) * 2 + bph) * 4 + b, 64, stride=32), :] for b in range(4)], axis=0
        )

    for mj in range(2):
        right = jnp.concatenate(
            [jnp.concatenate([rows_of(mj, p, 0), rows_of(mj, p, 1)], axis=1) for p in range(2)], axis=0
        )
        product = dot3((a2[0], a2[1]), halves(right), NN)

        @pl.when(s == 0)
        def _():
            total[mj] = product

        @pl.when(s > 0)
        def _():
            total[mj] += product

    @pl.when(s == 3)
    def _():
        pltpu.make_async_copy(closing, c, sem.at[2]).wait()
        for part in range(2):
            for half in range(2):
                tmp[half] = c[part, :, pl.ds(128 * half, 128)]
            for half in range(2):
                for b in range(4):
                    value = tmp[half, pl.ds(b, 64, stride=4), :]
                    at = 64 * b, 128 * half
                    if part == 0:
                        put(c2, pl.ds(at[0], 64), pl.ds(at[1], 128), value)
                        put(c2, pl.ds(256 + at[0], 64), pl.ds(256 + at[1], 128), value)
                    else:
                        put(c2, pl.ds(at[0], 64), pl.ds(256 + at[1], 128), value)
                        put(c2, pl.ds(256 + at[0], 64), pl.ds(at[1], 128), -value)
        for mj in range(2):
            left = jnp.concatenate([total[mj, :256], total[mj, 256:]], axis=1)
            result = dot3(halves(left), (c2[0], c2[1]), NN)
            for q in range(2):
                for half in range(2):
                    cols = 256 * q + 128 * half
                    out[pl.ds(1024 * q + 2 * half + mj, 256, stride=4), :] = result[:, cols : cols + 128]


SMEM = pl.BlockSpec(memory_space=pltpu.SMEM)
ANY = pl.BlockSpec(memory_space=pl.ANY)
PARAMS = pltpu.CompilerParams(vmem_limit_bytes=48 * 2**20)


def per_device(stems, slice_branches, closing, path, slice_assign):
    x = stems.reshape(2, 2048, 256)
    send = pl.pallas_call(
        before_kernel,
        grid=(8,),
        in_specs=[
            SMEM,
            SMEM,
            ANY,
            pl.BlockSpec((2, 2048, 128), lambda m: (0, 0, 0)),
            pl.BlockSpec((2, 2048, 128), lambda m: (0, 0, 1)),
        ],
        out_specs=pl.BlockSpec((2048, 128), lambda m: (m // 2, 0)),
        out_shape=jax.ShapeDtypeStruct((8192, 128), F32),
        scratch_shapes=[
            pltpu.VMEM((2, 2, 256, 256), F32),
            pltpu.VMEM((2, 256, 128), F32),
            pltpu.VMEM((2, 512, 512), BF),
            pltpu.VMEM((2, 512, 512), BF),
            pltpu.SemaphoreType.DMA((2,)),
        ],
        compiler_params=PARAMS,
        name="before",
    )(slice_assign, path, slice_branches, x, x)
    got = lax.all_to_all(send.reshape(256, 32, 128), ALL, 0, 0, tiled=True).reshape(8192, 128)
    out = pl.pallas_call(
        after_kernel,
        grid=(4,),
        in_specs=[SMEM, SMEM, ANY, ANY, pl.BlockSpec((2048, 128), lambda s: (s, 0))],
        out_specs=pl.BlockSpec((2048, 128), lambda s: (0, 0)),
        out_shape=jax.ShapeDtypeStruct((2048, 128), F32),
        scratch_shapes=[
            pltpu.VMEM((2, 2, 256, 256), F32),
            pltpu.VMEM((2, 256, 256), F32),
            pltpu.VMEM((2, 256, 128), F32),
            pltpu.VMEM((2, 512, 512), BF),
            pltpu.VMEM((2, 512, 512), BF),
            pltpu.VMEM((2, 512, 256), F32),
            pltpu.SemaphoreType.DMA((3,)),
        ],
        compiler_params=PARAMS,
        name="after",
    )(slice_assign, path, slice_branches, closing, got)
    out = out.reshape(2, 256, 2, 2, 128)
    return jnp.transpose(out, (0, 1, 3, 2, 4)).reshape(2, 256, 2, 256)


def solution(mesh):
    return jax.shard_map(
        per_device,
        mesh=mesh,
        in_specs=(P("cuts", None, "shard", None, None), P(), P(), P(), P()),
        out_specs=P(None, "shard", "cuts", None),
        check_vma=False,
    )
```

time: 405 us -> 149 us (0.37)
  waiting for transfers between devices: 186 us -> 0 us
  matrix products: 47.8 us -> 0 us
  Pallas kernels: 0 us -> 35.3 us
  between operations: 21.6 us -> 0.02 us
  local copies, waits for them, and re-layouts: 18 us -> 1.32 us
  starting transfers between devices: 15.4 us -> 0 us
  other arithmetic: 10.2 us -> 0 us
  blocking collectives: 102 us -> 112 us
    unnamed x2 -> x0, waiting for transfers between devices: 95 us -> none
    all_to_all x1 -> x0, waiting for transfers between devices: 90.6 us -> none  [per_device(): lax.all_to_all(field, 'shard', split_axis=1, concat_axis=1, tiled=True)]
    dot_general x4 -> x0, matrix products: 47.8 us -> none  [the longest x2 26.3 us: right_apply(): prod = jnp.einsum('plmk,qkn->pqlmn', field, matrix, precision=HIGH)]
    pallas_call x0 -> x2, Pallas kernels: none -> 35.3 us  [the longest x1 21.9 us: per_device(): pl.pallas_call(before_kernel, grid=(8,), in_specs=[SMEM, SMEM, ANY, pl.Bl...]
    all_to_all x1 -> x0, starting transfers between devices: 15.4 us -> none  [per_device(): lax.all_to_all(field, 'shard', split_axis=1, concat_axis=1, tiled=True)]
    another operation x2 -> x0, local copies, waits for them, and re-layouts: 11 us -> none  [the longest x1 5.49 us: right_apply(): return jnp.stack([prod[0, 0] - prod[1, 1], prod[0, 1] + prod[1, 0]])]
    all_to_all x1, blocking collectives: 102 us -> 112 us  [per_device(): lax.all_to_all(send.reshape(256, 32, 128), ALL, 0, 0, tiled=True)]
    another operation x3 -> x0, other arithmetic: 6.7 us -> none  [the longest x2 4.5 us: right_apply(): return jnp.stack([prod[0, 0] - prod[1, 1], prod[0, 1] + prod[1, 0]])]
  transfers between devices with their start and end apart: 2 -> 0, of which waited for: 2 -> 0; matrix products, arithmetic and copies ran while one was open for 0% -> 0% of each run, Pallas kernels for 0% -> 0%
where the time goes in v1:
time: 149 us
  blocking collectives  112 us (75%)
  Pallas kernels  35.3 us (24%)
    all_to_all x1, blocking collectives, per_device(): lax.all_to_all(send.reshape(256, 32, 128), ALL, 0, 0, tiled=True)  112 us
    pallas_call x1, Pallas kernels, per_device(): pl.pallas_call(before_kernel, grid=(8,), in_specs=[SMEM, SMEM, ANY, pl.Bl...  21.9 us
    pallas_call x1, Pallas kernels, per_device(): pl.pallas_call(after_kernel, grid=(4,), in_specs=[SMEM, SMEM, ANY, ANY, p...  13.4 us

profile of v1, /device:TPU:1, one launch (start us, length us, event | category | flops | bytes accessed | tf_op | source)
XLA Modules:
  0.0 148.7 jit_solution(15325044828533494951)
XLA Ops:
  0.0 0.0 copy-start.1
  0.0 0.7 copy-done.1
  0.7 0.0 copy-start.2
  0.7 0.7 copy-done.2
  1.3 21.9 %before.1 = f32[8192,128]{1,0:T(8,128)S(1)} custom-call(s32[6]{0:T(128)S(1)} %copy-done.1, s32[3]{0:T(128)S(1)} %copy-done.2, f32[6,3,2,256,256]{4,3,2,1,0:T(8,128)} %branches.3, f32[2,2048,256]{2,1,0:T(8,128)} %bitcast.10, f32[2,2048,256]{2,1,0:T(8,128)} %bitcast.11), custom_call_target="tpu_custom_call" | custom-call | tf_op jit(solution)/shard_map/before/pallas_call | solution.py:160
  23.2 0.0 copy-start
  23.2 112.1 %all_to_all.5 = f32[256,32,128]{2,1,0:T(8,128)S(1)} all-to-all(f32[256,32,128]{2,1,0:T(8,128)S(1)} %bitcast.9), channel_id=1, replica_groups=mesh['cuts'=4,'shard'=64] {'cuts','shard'}, dimensions={0} | all-to-all | bytes 8388608 | tf_op jit(solution)/shard_map/all_to_all | solution.py:182
  135.3 0.0 copy-done
  135.3 13.4 %after.1 = f32[2048,128]{1,0:T(8,128)} custom-call(s32[6]{0:T(128)S(1)} %copy-done.1, s32[3]{0:T(128)S(1)} %copy-done.2, f32[6,3,2,256,256]{4,3,2,1,0:T(8,128)} %branches.3, f32[2,256,256]{2,1,0:T(8,128)S(1)} %copy-done, f32[8192,128]{1,0:T(8,128)S(1)} %bitcast.8), custom_call_target="tpu_custom_call" | custom-call | tf_op jit(solution)/shard_map/after/pallas_call | solution.py:183
Async XLA Ops:
  0.0 0.7 copy-start.1
  0.7 0.7 copy-start.2
  23.2 112.1 %copy-start = (f32[2,256,256]{2,1,0:T(8,128)S(1)}, f32[2,256,256]{2,1,0:T(8,128)}, u32[]{:S(2)}) copy-start(f32[2,256,256]{2,1,0:T(8,128)} %closing.1) | copy-start | bytes 1572868

commit v2 on v0

v2 whole, which is shorter than its diff:
```python
import functools

import jax
import jax.numpy as jnp
from jax import lax
from jax.experimental import pallas as pl
from jax.experimental.pallas import tpu as pltpu
from jax.sharding import PartitionSpec as P

BF, F32 = jnp.bfloat16, jnp.float32
ALL = ("cuts", "shard")


def halves(x):
    high = x.astype(BF)
    return high, (x - high.astype(F32)).astype(BF)


def dot3(left, right):
    dot = functools.partial(jnp.dot, preferred_element_type=F32)
    rows = left.shape[0] // 2
    both = dot(left, right[0])
    return both[:rows] + (both[rows:] + dot(left[:rows], right[1]))


def stacked(x):
    return cat(halves(x), 0)


def put(pair, rows, cols, value):
    pair[0, rows, cols], pair[1, rows, cols] = halves(value)


def right_blocks(pair, part, value):
    one, two = slice(0, 256), slice(256, 512)
    if part == 0:
        put(pair, one, one, value)
        put(pair, two, two, value)
    else:
        put(pair, one, two, value)
        put(pair, two, one, -value)


def cat(pieces, axis):
    return jnp.concatenate(pieces, axis=axis)


def before_kernel(assign, path, branches, x, send, words, steps, xs, v, tmp, w1, w0, ys, word_sem, x_sem, v_sem, y_sem):
    words_in = [pltpu.make_async_copy(a, to, word_sem.at[i]) for i, (a, to) in enumerate(((assign, words), (path, steps)))]
    stem = [
        pltpu.make_async_copy(x.at[p, :, pl.ds(128 * h, 128)], xs.at[p, h], x_sem.at[p, h])
        for p in range(2)
        for h in range(2)
    ]
    for copy in words_in:
        copy.start()
    for copy in stem:
        copy.start()
    for copy in words_in:
        copy.wait()
    value = words[lax.axis_index("cuts")]
    weights = [pltpu.make_async_copy(branches.at[value, steps[i]], v.at[i], v_sem.at[i]) for i in (1, 0)]
    for copy in weights:
        copy.start()
    for copy, pair, index in zip(weights, (w1, w0), (1, 0), strict=True):
        copy.wait()
        for part in range(2):
            turned = v[index, part].T
            for h in range(2):
                tmp[h] = turned[:, 128 * h : 128 * h + 128]
            moved = [cat([tmp[h, pl.ds(b, 64, stride=4), :] for b in range(4)], 0) for h in range(2)]
            right_blocks(pair, part, cat(moved, 1).T)
    for copy in stem:
        copy.wait()
    low_lane = lax.broadcasted_iota(jnp.int32, (64, 128), 1) < 64

    def along_k(m):
        field = cat([xs[p, h, pl.ds(m, 256, stride=8), :] for p in range(2) for h in range(2)], 1)
        return dot3(stacked(field), (w1[0], w1[1]))

    later = along_k(0)
    for m in range(8):
        c, parity = m // 2, m % 2
        z = later
        if PIPELINED and m < 7:
            later = along_k(m + 1)
        z = cat([z[:, :256].T, z[:, 256:].T], 1)
        y = dot3(stacked(z), (w0[0], w0[1]))
        if not PIPELINED and m < 7:
            later = along_k(m + 1)
        for q in range(2):
            for bph in range(2):
                for bh in range(2):
                    cols = slice(256 * q + 128 * bh, 256 * q + 128 * bh + 128)
                    one = y[128 * bph : 128 * bph + 64, cols]
                    two = y[128 * bph + 64 : 128 * bph + 128, cols]
                    r = 2048 * c + 16 * parity + (q * 2 + bph) * 4 + bh * 2
                    ys[pl.ds(r, 64, stride=32), :] = jnp.where(low_lane, one, pltpu.roll(two, 64, 1))
                    ys[pl.ds(r + 1, 64, stride=32), :] = jnp.where(low_lane, pltpu.roll(one, 64, 1), two)
        if parity == 1:
            rows = pl.ds(2048 * c, 2048)
            pltpu.make_async_copy(ys.at[rows], send.at[rows], y_sem.at[c]).start()
    for c in range(4):
        rows = pl.ds(2048 * c, 2048)
        pltpu.make_async_copy(ys.at[rows], send.at[rows], y_sem.at[c]).wait()


def matrices_kernel(assign, path, branches, closing, a2, c2, v, c, tmp, v_sem, c_sem):
    copies = [
        pltpu.make_async_copy(
            branches.at[assign[s], path[2], p, :, pl.ds(128 * h, 128)], v.at[s, p, h], v_sem.at[s, p, h]
        )
        for s in range(4)
        for p in range(2)
        for h in range(2)
    ]
    last = pltpu.make_async_copy(closing, c, c_sem)
    for copy in copies:
        copy.start()
    last.start()
    for copy in copies:
        copy.wait()
    for s in range(4):
        for p in range(2):
            moved = [cat([v[s, p, h, pl.ds(b, 64, stride=4), :] for b in range(4)], 0) for h in range(2)]
            piece = cat(moved, 1).T
            one, two = slice(512 * s, 512 * s + 256), slice(512 * s + 256, 512 * s + 512)
            for at, cols, value in (
                ((0, one, piece), (256, two, piece)) if p == 0 else ((256, one, piece), (0, two, -piece))
            ):
                a2[at : at + 256, cols], a2[512 + at : 768 + at, cols] = halves(value)
    last.wait()
    for p in range(2):
        for h in range(2):
            tmp[h] = c[p, :, 128 * h : 128 * h + 128]
        moved = cat([cat([tmp[h, pl.ds(b, 64, stride=4), :] for b in range(4)], 0) for h in range(2)], 1)
        right_blocks(c2, p, moved)


def after_kernel(got, a2, c2, out, rs, a2s, r_sem, a_sem):
    def reads(s):
        rows = pl.ds(2048 * s, 2048)
        return (
            pltpu.make_async_copy(a2.at[:, pl.ds(512 * s, 512)], a2s.at[s], a_sem.at[s]),
            pltpu.make_async_copy(got.at[rows], rs.at[rows], r_sem.at[s]),
        )

    for s in range(4):
        for copy in reads(s):
            copy.start()
    total = None
    for s in range(4):
        for copy in reads(s):
            copy.wait()

        def sources(parity, p, bph):
            at = 2048 * s + 16 * parity + (p * 2 + bph) * 4
            return cat([rs[pl.ds(at + b, 64, stride=32), :] for b in range(4)], 0)

        right = cat(
            [cat([sources(parity, p, bph) for parity in range(2) for bph in range(2)], 1) for p in range(2)], 0
        )
        term = dot3(a2s[s], halves(right))
        total = term if total is None else total + term
    left = cat([cat([total[:256, cols], total[256:, cols]], 1) for cols in (slice(0, 256), slice(256, 512))], 0)
    result = dot3(stacked(left), (c2[0], c2[1]))
    for parity in range(2):
        for q in range(2):
            for h in range(2):
                cols = slice(256 * q + 128 * h, 256 * q + 128 * h + 128)
                out[pl.ds(1024 * q + 2 * h + parity, 256, stride=4), :] = result[256 * parity : 256 * parity + 256, cols]


PIPELINED = True
SMEM = pl.BlockSpec(memory_space=pltpu.SMEM)
HBM = pl.BlockSpec(memory_space=pltpu.HBM)
VMEM = pl.BlockSpec(memory_space=pltpu.VMEM)
DMA = pltpu.SemaphoreType.DMA


def kernel_call(kernel, in_specs, out_specs, shapes, operands, name, scratch, mib):
    return pl.pallas_call(
        kernel,
        in_specs=in_specs,
        out_specs=out_specs,
        out_shape=shapes,
        scratch_shapes=scratch,
        compiler_params=pltpu.CompilerParams(vmem_limit_bytes=mib * 2**20),
        name=name,
    )(*operands)


def shaped(*shape, dtype=F32):
    return jax.ShapeDtypeStruct(shape, dtype)


def before(operands):
    return kernel_call(
        before_kernel,
        [HBM] * 4,
        [HBM],
        [pltpu.HBM((8192, 128), F32)],
        operands,
        "before",
        [
            pltpu.SMEM((6,), jnp.int32),
            pltpu.SMEM((3,), jnp.int32),
            pltpu.VMEM((2, 2, 2048, 128), F32),
            pltpu.VMEM((2, 2, 256, 256), F32),
            pltpu.VMEM((2, 256, 128), F32),
            pltpu.VMEM((2, 512, 512), BF),
            pltpu.VMEM((2, 512, 512), BF),
            pltpu.VMEM((8192, 128), F32),
            DMA((2,)),
            DMA((2, 2)),
            DMA((2,)),
            DMA((4,)),
        ],
        32,
    )[0]


def matrices(operands):
    return kernel_call(
        matrices_kernel,
        [SMEM, SMEM, HBM, HBM],
        [VMEM, VMEM],
        [pltpu.HBM((1024, 2048), BF), shaped(2, 512, 512, dtype=BF)],
        operands,
        "matrices",
        [
            pltpu.VMEM((4, 2, 2, 256, 128), F32),
            pltpu.VMEM((2, 256, 256), F32),
            pltpu.VMEM((2, 256, 128), F32),
            DMA((4, 2, 2)),
            DMA,
        ],
        24,
    )


def after(got, a2, c2):
    return kernel_call(
        after_kernel,
        [HBM, HBM, VMEM],
        [VMEM],
        [shaped(2048, 128)],
        (got, a2, c2),
        "after",
        [pltpu.VMEM((8192, 128), F32), pltpu.VMEM((4, 1024, 512), BF), DMA((4,)), DMA((4,))],
        32,
    )[0]


def in_hbm(a):
    return pltpu.with_memory_space_constraint(a, pltpu.HBM)


def per_device(stems, slice_branches, closing, path, slice_assign):
    branches = in_hbm(slice_branches)
    send = before((in_hbm(slice_assign), in_hbm(path), branches, in_hbm(stems.reshape(2, 2048, 256))))
    a2, c2 = matrices((slice_assign, path, branches, in_hbm(closing)))
    got = lax.all_to_all(send.reshape(256, 32, 128), ALL, 0, 0, tiled=True).reshape(8192, 128)
    out = after(in_hbm(got), in_hbm(a2), c2)
    out = out.reshape(2, 256, 2, 2, 128)
    return jnp.transpose(out, (0, 1, 3, 2, 4)).reshape(2, 256, 2, 256)


def solution(mesh):
    return jax.shard_map(
        per_device,
        mesh=mesh,
        in_specs=(P("cuts", None, "shard", None, None), P(), P(), P(), P()),
        out_specs=P(None, "shard", "cuts", None),
        check_vma=False,
    )
```

time: 405 us -> 136 us (0.34)
  blocking collectives: 102 us -> 0 us
  waiting for transfers between devices: 186 us -> 90.8 us
  matrix products: 47.8 us -> 0 us
  Pallas kernels: 0 us -> 27.7 us
  between operations: 21.6 us -> 0.22 us
  local copies, waits for them, and re-layouts: 18 us -> 0.01 us
  other arithmetic: 10.2 us -> 0 us
    all_to_all x1 -> x0, blocking collectives: 102 us -> none  [per_device(): lax.all_to_all(field, 'shard', split_axis=3, concat_axis=3, tiled=True)]
    unnamed x2 -> x0, waiting for transfers between devices: 95 us -> none
    dot_general x4 -> x0, matrix products: 47.8 us -> none  [the longest x2 26.3 us: right_apply(): prod = jnp.einsum('plmk,qkn->pqlmn', field, matrix, precision=HIGH)]
    pallas_call x0 -> x3, Pallas kernels: none -> 27.7 us  [kernel_call(): pl.pallas_call(kernel, in_specs=in_specs, out_specs=out_specs, out_shape=...]
    another operation x2 -> x0, local copies, waits for them, and re-layouts: 11 us -> none  [the longest x1 5.49 us: right_apply(): return jnp.stack([prod[0, 0] - prod[1, 1], prod[0, 1] + prod[1, 0]])]
    another operation x3 -> x0, other arithmetic: 6.7 us -> none  [the longest x2 4.5 us: right_apply(): return jnp.stack([prod[0, 0] - prod[1, 1], prod[0, 1] + prod[1, 0]])]
  transfers between devices with their start and end apart: 2 -> 1, of which waited for: 2 -> 1; matrix products, arithmetic and copies ran while one was open for 0% -> 0% of each run, Pallas kernels for 0% -> 4%
where the time goes in v2:
time: 136 us; the launch traced here: 135 us
  waiting for transfers between devices  90.8 us (67%)
  Pallas kernels  27.7 us (20%)
  starting transfers between devices  16.7 us (12%)
    all_to_all x1, waiting for transfers between devices, per_device(): lax.all_to_all(send.reshape(256, 32, 128), ALL, 0, 0, tiled=True)  90.8 us
    pallas_call x3, Pallas kernels, kernel_call(): pl.pallas_call(kernel, in_specs=in_specs, out_specs=out_specs, out_shape=...  27.7 us
    all_to_all x1, starting transfers between devices, per_device(): lax.all_to_all(send.reshape(256, 32, 128), ALL, 0, 0, tiled=True)  16.7 us
  transfers between devices with their start and end apart: 1, of which 1 were waited for; matrix products, arithmetic and copies ran while one was open for 0% of the time, Pallas kernels for 4%

profile of v2, /device:TPU:1, one launch (start us, length us, event | category | flops | bytes accessed | tf_op | source)
XLA Modules:
  0.0 135.3 jit_solution(1394066527648385022)
XLA Ops:
  0.0 14.5 %before.1 = f32[8192,128]{1,0:T(8,128)} custom-call(s32[6]{0:T(128)} %assign.3, s32[3]{0:T(128)} %path.3, f32[6,3,2,256,256]{4,3,2,1,0:T(8,128)} %branches.3, f32[2,2048,256]{2,1,0:T(8,128)} %bitcast.9), custom_call_target="tpu_custom_call" | custom-call | tf_op jit(solution)/shard_map/before/pallas_call | solution.py:182
  14.5 0.0 copy-start
  14.5 0.0 copy-start.1
  14.5 16.7 %all-to-all-start = ((f32[256,32,128]{2,1,0:T(8,128)}), f32[256,32,128]{2,1,0:T(8,128)}, u32[]{:S(2)}, u32[]{:S(2)}) async-start(f32[256,32,128]{2,1,0:T(8,128)} %bitcast.8), calls=%async_computation | async-start | bytes 8388608 | tf_op jit(solution)/shard_map/all_to_all | solution.py:263
  31.2 0.0 copy-done
  31.2 0.0 copy-done.1
  31.2 4.9 %matrices.1 = (bf16[1024,2048]{1,0:T(8,128)(2,1)}, bf16[2,512,512]{2,1,0:T(8,128)(2,1)S(1)}) custom-call(s32[6]{0:T(128)S(1)} %copy-done, s32[3]{0:T(128)S(1)} %copy-done.1, f32[6,3,2,256,256]{4,3,2,1,0:T(8,128)} %branches.3, f32[2,256,256]{2,1,0:T(8,128)} %closing.1), custom_call_target="tpu_custom_call" | custom-call | tf_op jit(solution)/shard_map/matrices/pallas_call | solution.py:182
  36.1 90.8 %all-to-all-done = f32[256,32,128]{2,1,0:T(8,128)} async-done(((f32[256,32,128]{2,1,0:T(8,128)}), f32[256,32,128]{2,1,0:T(8,128)}, u32[]{:S(2)}, u32[]{:S(2)}) %all-to-all-start) | async-done | bytes 4194336 | tf_op jit(solution)/shard_map/all_to_all | solution.py:263
  126.9 8.3 %after.1 = f32[2048,128]{1,0:T(8,128)} custom-call(f32[8192,128]{1,0:T(8,128)} %bitcast.2.got, bf16[1024,2048]{1,0:T(8,128)(2,1)} %get-tuple-element.7.a2, bf16[2,512,512]{2,1,0:T(8,128)(2,1)S(1)} %get-tuple-element.8.c2), custom_call_target="tpu_custom_call" | custom-call | tf_op jit(solution)/shard_map/after/pallas_call | solution.py:182
Async XLA Ops:
  14.5 16.7 %copy-start = (s32[6]{0:T(128)S(1)}, s32[6]{0:T(128)}, u32[]{:S(2)}) copy-start(s32[6]{0:T(128)} %assign.3) | copy-start | bytes 76
  14.5 16.7 %copy-start.1 = (s32[3]{0:T(128)S(1)}, s32[3]{0:T(128)}, u32[]{:S(2)}) copy-start(s32[3]{0:T(128)} %path.3) | copy-start | bytes 40
  14.5 112.4 %all-to-all-start = ((f32[256,32,128]{2,1,0:T(8,128)}), f32[256,32,128]{2,1,0:T(8,128)}, u32[]{:S(2)}, u32[]{:S(2)}) async-start(f32[256,32,128]{2,1,0:T(8,128)} %bitcast.8), calls=%async_computation | async-start | bytes 8388608 | tf_op jit(solution)/shard_map/all_to_all | solution.py:263

commit v3 on v2

v3 whole, which is shorter than its diff:
```python
import functools

import jax
import jax.numpy as jnp
from jax import lax
from jax.experimental import pallas as pl
from jax.experimental.pallas import tpu as pltpu
from jax.sharding import PartitionSpec as P

BF, F32 = jnp.bfloat16, jnp.float32
ALL = ("cuts", "shard")


def halves(x):
    high = x.astype(BF)
    return high, (x - high.astype(F32)).astype(BF)


def dot3(left, right):
    dot = functools.partial(jnp.dot, preferred_element_type=F32)
    rows = left.shape[0] // 2
    both = dot(left, right[0])
    return both[:rows] + (both[rows:] + dot(left[:rows], right[1]))


def stacked(x):
    return cat(halves(x), 0)


def put(pair, rows, cols, value):
    pair[0, rows, cols], pair[1, rows, cols] = halves(value)


def right_blocks(pair, part, value):
    one, two = slice(0, 256), slice(256, 512)
    if part == 0:
        put(pair, one, one, value)
        put(pair, two, two, value)
    else:
        put(pair, one, two, value)
        put(pair, two, one, -value)


def cat(pieces, axis):
    return jnp.concatenate(pieces, axis=axis)


def before_kernel(assign, path, branches, x, send, words, steps, xs, v, tmp, mix, w1, w0, ys, word_sem, x_sem, v_sem, y_sem):
    words_in = [pltpu.make_async_copy(a, to, word_sem.at[i]) for i, (a, to) in enumerate(((assign, words), (path, steps)))]
    stem = [
        pltpu.make_async_copy(x.at[p, :, pl.ds(128 * h, 128)], xs.at[p, h], x_sem.at[p, h])
        for p in range(2)
        for h in range(2)
    ]
    for copy in words_in:
        copy.start()
    for copy in stem:
        copy.start()
    for copy in words_in:
        copy.wait()
    value = words[lax.axis_index("cuts")]
    turn_by = lax.rem(lax.axis_index("shard"), 8)
    weights = [pltpu.make_async_copy(branches.at[value, steps[i]], v.at[i], v_sem.at[i]) for i in range(2)]
    for copy in (weights[1], weights[0]):
        copy.start()

    def turn(index, part):
        turned = v[index, part].T
        for h in range(2):
            tmp[h] = turned[:, 128 * h : 128 * h + 128]

    weights[1].wait()
    for part in range(2):
        turn(1, part)
        for h in range(2):
            for b in range(4):
                value = tmp[h, pl.ds(b, 64, stride=4), :]
                mix[h, pl.ds(lax.rem(b + 4 * part + turn_by, 8), 64, stride=8), :] = value
                mix[2 + h, pl.ds(lax.rem(b + 4 * (1 - part) + turn_by, 8), 64, stride=8), :] = -value if part else value
    for h in range(4):
        put(w1, slice(128 * h, 128 * h + 128), slice(0, 512), mix[h].T)

    for copy in stem:
        copy.wait()

    def along_k(m):
        field = cat([xs[p, h, pl.ds(m, 256, stride=8), :] for p in range(2) for h in range(2)], 1)
        return dot3(stacked(field), (w1[0], w1[1]))

    later = along_k(0)
    weights[0].wait()
    for part in range(2):
        turn(0, part)
        moved = [cat([tmp[h, pl.ds(b, 64, stride=4), :] for b in range(4)], 0) for h in range(2)]
        put(w0, slice(0, 256), slice(256 * part, 256 * part + 256), cat(moved, 1).T)
    imaginary = lax.rem(lax.broadcasted_iota(jnp.int32, (64, 8, 256), 1) + (8 - turn_by), 8) >= 4
    for m in range(8):
        c, parity = m // 2, m % 2
        z = later
        if m < 7:
            later = along_k(m + 1)
        u = dot3(stacked(z.T), (w0[0], w0[1])).reshape(64, 8, 512)
        across = pltpu.roll(u[:, :, 256:], 4, 1)
        y = u[:, :, :256] + jnp.where(imaginary, across, -across)
        for bh in range(2):
            r = 16 * parity + 8 * bh
            ys[64 * c : 64 * c + 64, r : r + 8, :] = y[:, :, 128 * bh : 128 * bh + 128]
        if parity == 1:
            rows = pl.ds(64 * c, 64)
            pltpu.make_async_copy(ys.at[rows], send.at[rows], y_sem.at[c]).start()
    for c in range(4):
        rows = pl.ds(64 * c, 64)
        pltpu.make_async_copy(ys.at[rows], send.at[rows], y_sem.at[c]).wait()


def matrices_kernel(assign, path, branches, closing, a2, c2, v, c, tmp, v_sem, c_sem):
    copies = [
        pltpu.make_async_copy(
            branches.at[assign[s], path[2], p, :, pl.ds(128 * h, 128)], v.at[s, p, h], v_sem.at[s, p, h]
        )
        for s in range(4)
        for p in range(2)
        for h in range(2)
    ]
    last = pltpu.make_async_copy(closing, c, c_sem)
    for copy in copies:
        copy.start()
    last.start()
    for copy in copies:
        copy.wait()
    for s in range(4):
        for p in range(2):
            moved = [cat([v[s, p, h, pl.ds(b, 64, stride=4), :] for b in range(4)], 0) for h in range(2)]
            at = 256 * p
            a2[s, at : at + 256, :], a2[s, 512 + at : 768 + at, :] = halves(cat(moved, 1).T)
    last.wait()
    for p in range(2):
        for h in range(2):
            tmp[h] = c[p, :, 128 * h : 128 * h + 128]
        moved = cat([cat([tmp[h, pl.ds(b, 64, stride=4), :] for b in range(4)], 0) for h in range(2)], 1)
        right_blocks(c2, p, moved)


def after_kernel(got, a2, c2, out, rs, r_sem):
    def read(s):
        rows = pl.ds(2048 * s, 2048)
        return pltpu.make_async_copy(got.at[rows], rs.at[s, pl.ds(8, 2048)], r_sem.at[s])

    w = lax.broadcasted_iota(jnp.int32, (8, 128), 0)

    def row_of(s, block, j):
        rows = []
        for z in range(8):
            at = 256 * z + 8 * block + j + 8
            straight = rs[s, pl.ds(at, 8, stride=33), :]
            rows.append(jnp.where(w + j < 8, straight, rs[s, pl.ds(at - 8, 8, stride=33), :]) if j else straight)
        return cat(rows, 0)

    low_lane = lax.broadcasted_iota(jnp.int32, (64, 128), 1) < 64

    def sources(s, p, parity, bph):
        rows = []
        for bh in range(2):
            one, two = (row_of(s, 2 * parity + bh, 4 * p + 2 * bph + bpl) for bpl in range(2))
            crossed = pltpu.roll(jnp.where(low_lane, two, one), 64, 1)
            rows += [jnp.where(low_lane, one, crossed), jnp.where(low_lane, crossed, two)]
        return cat(rows, 0)

    def arrived(s):
        read(s).wait()
        return halves(cat([sources(s, p, m, bph) for p in range(2) for m in range(2) for bph in range(2)], 1))

    for s in range(4):
        read(s).start()
        rs[s, 0:8] = rs[s, 2056:2064] = jnp.zeros((8, 128), F32)
    later, total = arrived(0), None
    for s in range(4):
        right = later
        if s < 3:
            later = arrived(s + 1)
        term = dot3(a2[s], right)
        total = term if total is None else total + term
    real = total[:256, :512] - total[256:, 512:]
    imaginary = total[256:, :512] + total[:256, 512:]
    left = cat([cat([real[:, cols], imaginary[:, cols]], 1) for cols in (slice(0, 256), slice(256, 512))], 0)
    result = dot3(stacked(left), (c2[0], c2[1]))
    for parity in range(2):
        for q in range(2):
            for h in range(2):
                cols = slice(256 * q + 128 * h, 256 * q + 128 * h + 128)
                out[pl.ds(1024 * q + 2 * h + parity, 256, stride=4), :] = result[256 * parity : 256 * parity + 256, cols]


SMEM = pl.BlockSpec(memory_space=pltpu.SMEM)
HBM = pl.BlockSpec(memory_space=pltpu.HBM)
VMEM = pl.BlockSpec(memory_space=pltpu.VMEM)
DMA = pltpu.SemaphoreType.DMA


def kernel_call(kernel, in_specs, out_specs, shapes, operands, name, scratch, mib):
    return pl.pallas_call(
        kernel,
        in_specs=in_specs,
        out_specs=out_specs,
        out_shape=shapes,
        scratch_shapes=scratch,
        compiler_params=pltpu.CompilerParams(vmem_limit_bytes=mib * 2**20),
        name=name,
    )(*operands)


def shaped(*shape, dtype=F32):
    return jax.ShapeDtypeStruct(shape, dtype)


def before(operands):
    return kernel_call(
        before_kernel,
        [HBM] * 4,
        [HBM],
        [pltpu.HBM((256, 32, 128), F32)],
        operands,
        "before",
        [
            pltpu.SMEM((6,), jnp.int32),
            pltpu.SMEM((3,), jnp.int32),
            pltpu.VMEM((2, 2, 2048, 128), F32),
            pltpu.VMEM((2, 2, 256, 256), F32),
            pltpu.VMEM((2, 256, 128), F32),
            pltpu.VMEM((4, 512, 128), F32),
            pltpu.VMEM((2, 512, 512), BF),
            pltpu.VMEM((2, 256, 512), BF),
            pltpu.VMEM((256, 32, 128), F32),
            DMA((2,)),
            DMA((2, 2)),
            DMA((2,)),
            DMA((4,)),
        ],
        32,
    )[0]


def matrices(operands):
    return kernel_call(
        matrices_kernel,
        [SMEM, SMEM, HBM, HBM],
        [VMEM, VMEM],
        [shaped(4, 1024, 256, dtype=BF), shaped(2, 512, 512, dtype=BF)],
        operands,
        "matrices",
        [
            pltpu.VMEM((4, 2, 2, 256, 128), F32),
            pltpu.VMEM((2, 256, 256), F32),
            pltpu.VMEM((2, 256, 128), F32),
            DMA((4, 2, 2)),
            DMA,
        ],
        24,
    )


def after(got, a2, c2):
    return kernel_call(
        after_kernel,
        [HBM, VMEM, VMEM],
        [VMEM],
        [shaped(2048, 128)],
        (got, a2, c2),
        "after",
        [pltpu.VMEM((4, 2064, 128), F32), DMA((4,))],
        28,
    )[0]


def in_hbm(a):
    return pltpu.with_memory_space_constraint(a, pltpu.HBM)


def per_device(stems, slice_branches, closing, path, slice_assign):
    branches = in_hbm(slice_branches)
    send = before((in_hbm(slice_assign), in_hbm(path), branches, in_hbm(stems.reshape(2, 2048, 256))))
    a2, c2 = matrices((slice_assign, path, branches, in_hbm(closing)))
    got = lax.all_to_all(send, ALL, 0, 0, tiled=True).reshape(8192, 128)
    out = after(in_hbm(got), a2, c2)
    out = out.reshape(2, 256, 2, 2, 128)
    return jnp.transpose(out, (0, 1, 3, 2, 4)).reshape(2, 256, 2, 256)


def solution(mesh):
    return jax.shard_map(
        per_device,
        mesh=mesh,
        in_specs=(P("cuts", None, "shard", None, None), P(), P(), P(), P()),
        out_specs=P(None, "shard", "cuts", None),
        check_vma=False,
    )
```

time: 136 us -> 131 us (0.963)
  Pallas kernels: 27.7 us -> 21.5 us
  waiting for transfers between devices: 90.8 us -> 92.6 us
    pallas_call x3, Pallas kernels: 27.7 us -> 21.5 us  [kernel_call(): pl.pallas_call(kernel, in_specs=in_specs, out_specs=out_specs, out_shape=...]
    all_to_all x1, waiting for transfers between devices: 90.8 us -> 92.6 us  [per_device(): got = lax.all_to_all(send, ALL, 0, 0, tiled=True).reshape(8192, 128)]
  transfers between devices with their start and end apart: 1 -> 1, of which waited for: 1 -> 1; matrix products, arithmetic and copies ran while one was open for 0% -> 0% of each run, Pallas kernels for 4% -> 2%
where the time goes in v3:
time: 131 us
  waiting for transfers between devices  92.6 us (71%)
  Pallas kernels  21.5 us (16%)
  starting transfers between devices  16.7 us (13%)
    all_to_all x1, waiting for transfers between devices, per_device(): got = lax.all_to_all(send, ALL, 0, 0, tiled=True).reshape(8192, 128)  92.6 us
    pallas_call x3, Pallas kernels, kernel_call(): pl.pallas_call(kernel, in_specs=in_specs, out_specs=out_specs, out_shape=...  21.5 us
    all_to_all x1, starting transfers between devices, per_device(): got = lax.all_to_all(send, ALL, 0, 0, tiled=True).reshape(8192, 128)  16.7 us
  transfers between devices with their start and end apart: 1, of which 1 were waited for; matrix products, arithmetic and copies ran while one was open for 0% of the time, Pallas kernels for 2%

profile of v3, /device:TPU:1, one launch (start us, length us, event | category | flops | bytes accessed | tf_op | source)
XLA Modules:
  0.0 130.8 jit_solution(8795594861260801499)
XLA Ops:
  0.0 11.3 %before.1 = f32[256,32,128]{2,1,0:T(8,128)} custom-call(s32[6]{0:T(128)} %assign.3, s32[3]{0:T(128)} %path.3, f32[6,3,2,256,256]{4,3,2,1,0:T(8,128)} %branches.3, f32[2,2048,256]{2,1,0:T(8,128)} %bitcast.7), custom_call_target="tpu_custom_call" | custom-call | tf_op jit(solution)/shard_map/before/pallas_call | solution.py:201
  11.3 0.0 copy-start
  11.3 0.0 copy-start.1
  11.3 16.7 %all-to-all-start = ((f32[256,32,128]{2,1,0:T(8,128)}), f32[256,32,128]{2,1,0:T(8,128)}, u32[]{:S(2)}, u32[]{:S(2)}) async-start(f32[256,32,128]{2,1,0:T(8,128)} %before.1), calls=%async_computation | async-start | bytes 8388608 | tf_op jit(solution)/shard_map/all_to_all | solution.py:283
  28.0 0.0 copy-done
  28.0 0.0 copy-done.1
  28.0 3.1 %matrices.1 = (bf16[4,1024,256]{2,1,0:T(8,128)(2,1)S(1)}, bf16[2,512,512]{2,1,0:T(8,128)(2,1)S(1)}) custom-call(s32[6]{0:T(128)S(1)} %copy-done, s32[3]{0:T(128)S(1)} %copy-done.1, f32[6,3,2,256,256]{4,3,2,1,0:T(8,128)} %branches.3, f32[2,256,256]{2,1,0:T(8,128)} %closing.1), custom_call_target="tpu_custom_call" | custom-call | tf_op jit(solution)/shard_map/matrices/pallas_call | solution.py:201
  31.1 92.6 %all-to-all-done = f32[256,32,128]{2,1,0:T(8,128)} async-done(((f32[256,32,128]{2,1,0:T(8,128)}), f32[256,32,128]{2,1,0:T(8,128)}, u32[]{:S(2)}, u32[]{:S(2)}) %all-to-all-start) | async-done | bytes 4194336 | tf_op jit(solution)/shard_map/all_to_all | solution.py:283
  123.7 7.1 %after.1 = f32[2048,128]{1,0:T(8,128)} custom-call(f32[8192,128]{1,0:T(8,128)} %bitcast.1.got, bf16[4,1024,256]{2,1,0:T(8,128)(2,1)S(1)} %get-tuple-element.7.a2, bf16[2,512,512]{2,1,0:T(8,128)(2,1)S(1)} %get-tuple-element.8.c2), custom_call_target="tpu_custom_call" | custom-call | tf_op jit(solution)/shard_map/after/pallas_call | solution.py:201
Async XLA Ops:
  11.3 16.7 %copy-start = (s32[6]{0:T(128)S(1)}, s32[6]{0:T(128)}, u32[]{:S(2)}) copy-start(s32[6]{0:T(128)} %assign.3) | copy-start | bytes 76
  11.3 16.7 %copy-start.1 = (s32[3]{0:T(128)S(1)}, s32[3]{0:T(128)}, u32[]{:S(2)}) copy-start(s32[3]{0:T(128)} %path.3) | copy-start | bytes 40
  11.3 112.4 %all-to-all-start = ((f32[256,32,128]{2,1,0:T(8,128)}), f32[256,32,128]{2,1,0:T(8,128)}, u32[]{:S(2)}, u32[]{:S(2)}) async-start(f32[256,32,128]{2,1,0:T(8,128)} %before.1), calls=%async_computation | async-start | bytes 8388608 | tf_op jit(solution)/shard_map/all_to_all | solution.py:283

commit v4 on v3

--- a/solution.py
+++ b/solution.py
@@ -87,7 +87,11 @@
         field = cat([xs[p, h, pl.ds(m, 256, stride=8), :] for p in range(2) for h in range(2)], 1)
         return dot3(stacked(field), (w1[0], w1[1]))
 
-    later = along_k(0)
+    def write(m):
+        where = pl.ds(64 * (m // 2), 64), pl.ds(16 * (m % 2), 16)
+        return pltpu.make_async_copy(ys.at[where], send.at[where], y_sem.at[m])
+
+    later = [along_k(0), along_k(1)]
     weights[0].wait()
     for part in range(2):
         turn(0, part)
@@ -96,21 +100,18 @@
     imaginary = lax.rem(lax.broadcasted_iota(jnp.int32, (64, 8, 256), 1) + (8 - turn_by), 8) >= 4
     for m in range(8):
         c, parity = m // 2, m % 2
-        z = later
-        if m < 7:
-            later = along_k(m + 1)
+        z = later.pop(0)
+        if m < 6:
+            later.append(along_k(m + 2))
         u = dot3(stacked(z.T), (w0[0], w0[1])).reshape(64, 8, 512)
         across = pltpu.roll(u[:, :, 256:], 4, 1)
         y = u[:, :, :256] + jnp.where(imaginary, across, -across)
         for bh in range(2):
             r = 16 * parity + 8 * bh
             ys[64 * c : 64 * c + 64, r : r + 8, :] = y[:, :, 128 * bh : 128 * bh + 128]
-        if parity == 1:
-            rows = pl.ds(64 * c, 64)
-            pltpu.make_async_copy(ys.at[rows], send.at[rows], y_sem.at[c]).start()
-    for c in range(4):
-        rows = pl.ds(64 * c, 64)
-        pltpu.make_async_copy(ys.at[rows], send.at[rows], y_sem.at[c]).wait()
+        write(m).start()
+    for m in range(8):
+        write(m).wait()
 
 
 def matrices_kernel(assign, path, branches, closing, a2, c2, v, c, tmp, v_sem, c_sem):
@@ -141,7 +142,7 @@
         right_blocks(c2, p, moved)
 
 
-def after_kernel(got, a2, c2, out, rs, r_sem):
+def after_kernel(got, a2, c2, out, rs, os, r_sem, o_sem):
     def read(s):
         rows = pl.ds(2048 * s, 2048)
         return pltpu.make_async_copy(got.at[rows], rs.at[s, pl.ds(8, 2048)], r_sem.at[s])
@@ -168,7 +169,8 @@
 
     def arrived(s):
         read(s).wait()
-        return halves(cat([sources(s, p, m, bph) for p in range(2) for m in range(2) for bph in range(2)], 1))
+        re, im = (cat([sources(s, p, m, bph) for m in range(2) for bph in range(2)], 1) for p in range(2))
+        return halves(re), halves(re + im), halves(im - re)
 
     for s in range(4):
         read(s).start()
@@ -178,17 +180,26 @@
         right = later
         if s < 3:
             later = arrived(s + 1)
-        term = dot3(a2[s], right)
-        total = term if total is None else total + term
-    real = total[:256, :512] - total[256:, 512:]
-    imaginary = total[256:, :512] + total[:256, 512:]
+        parts = [a2[s, 256 * i : 256 * i + 256] for i in range(4)]
+        both = parts[0].astype(F32) + parts[2].astype(F32) + (parts[1].astype(F32) + parts[3].astype(F32))
+        lefts = stacked(both), cat(parts[1::2], 0), cat(parts[::2], 0)
+        terms = [dot3(*pair) for pair in zip(lefts, right, strict=True)]
+        total = terms if total is None else [a + b for a, b in zip(total, terms, strict=True)]
+    real, imaginary = total[0] - total[1], total[0] + total[2]
     left = cat([cat([real[:, cols], imaginary[:, cols]], 1) for cols in (slice(0, 256), slice(256, 512))], 0)
-    result = dot3(stacked(left), (c2[0], c2[1]))
-    for parity in range(2):
-        for q in range(2):
+    left = stacked(left)
+    writes = []
+    for q in range(2):
+        result = dot3(left, (c2[0, :, 256 * q : 256 * q + 256], c2[1, :, 256 * q : 256 * q + 256]))
+        for parity in range(2):
             for h in range(2):
-                cols = slice(256 * q + 128 * h, 256 * q + 128 * h + 128)
-                out[pl.ds(1024 * q + 2 * h + parity, 256, stride=4), :] = result[256 * parity : 256 * parity + 256, cols]
+                value = result[256 * parity : 256 * parity + 256, 128 * h : 128 * h + 128]
+                os[pl.ds(1024 * q + 2 * h + parity, 256, stride=4), :] = value
+        rows = pl.ds(1024 * q, 1024)
+        writes.append(pltpu.make_async_copy(os.at[rows], out.at[rows], o_sem.at[q]))
+        writes[q].start()
+    for copy in writes:
+        copy.wait()
 
 
 SMEM = pl.BlockSpec(memory_space=pltpu.SMEM)
@@ -234,7 +245,7 @@
             DMA((2,)),
             DMA((2, 2)),
             DMA((2,)),
-            DMA((4,)),
+            DMA((8,)),
         ],
         32,
     )[0]
@@ -263,11 +274,11 @@
     return kernel_call(
         after_kernel,
         [HBM, VMEM, VMEM],
-        [VMEM],
-        [shaped(2048, 128)],
+        [HBM],
+        [pltpu.HBM((2048, 128), F32)],
         (got, a2, c2),
         "after",
-        [pltpu.VMEM((4, 2064, 128), F32), DMA((4,))],
+        [pltpu.VMEM((4, 2064, 128), F32), pltpu.VMEM((2048, 128), F32), DMA((4,)), DMA((2,))],
         28,
     )[0]
 

time: 131 us -> 130 us (level)
  no operation moved by 1% of the time
where the time goes in v4:
time: 130 us
  waiting for transfers between devices  92.6 us (71%)
  Pallas kernels  20.8 us (16%)
  starting transfers between devices  16.7 us (13%)
    all_to_all x1, waiting for transfers between devices, per_device(): got = lax.all_to_all(send, ALL, 0, 0, tiled=True).reshape(8192, 128)  92.6 us
    pallas_call x3, Pallas kernels, kernel_call(): pl.pallas_call(kernel, in_specs=in_specs, out_specs=out_specs, out_shape=...  20.8 us
    all_to_all x1, starting transfers between devices, per_device(): got = lax.all_to_all(send, ALL, 0, 0, tiled=True).reshape(8192, 128)  16.7 us
  transfers between devices with their start and end apart: 1, of which 1 were waited for; matrix products, arithmetic and copies ran while one was open for 0% of the time, Pallas kernels for 2%

profile of v4, /device:TPU:1, one launch (start us, length us, event | category | flops | bytes accessed | tf_op | source)
XLA Modules:
  0.0 130.3 jit_solution(10820946936810679134)
XLA Ops:
  0.0 11.2 %before.1 = f32[256,32,128]{2,1,0:T(8,128)} custom-call(s32[6]{0:T(128)} %assign.3, s32[3]{0:T(128)} %path.3, f32[6,3,2,256,256]{4,3,2,1,0:T(8,128)} %branches.3, f32[2,2048,256]{2,1,0:T(8,128)} %bitcast.7), custom_call_target="tpu_custom_call" | custom-call | tf_op jit(solution)/shard_map/before/pallas_call | solution.py:212
  11.2 0.0 copy-start
  11.2 0.0 copy-start.1
  11.2 16.7 %all-to-all-start = ((f32[256,32,128]{2,1,0:T(8,128)}), f32[256,32,128]{2,1,0:T(8,128)}, u32[]{:S(2)}, u32[]{:S(2)}) async-start(f32[256,32,128]{2,1,0:T(8,128)} %before.1), calls=%async_computation | async-start | bytes 8388608 | tf_op jit(solution)/shard_map/all_to_all | solution.py:294
  27.9 0.0 copy-done
  27.9 0.0 copy-done.1
  27.9 3.1 %matrices.1 = (bf16[4,1024,256]{2,1,0:T(8,128)(2,1)S(1)}, bf16[2,512,512]{2,1,0:T(8,128)(2,1)S(1)}) custom-call(s32[6]{0:T(128)S(1)} %copy-done, s32[3]{0:T(128)S(1)} %copy-done.1, f32[6,3,2,256,256]{4,3,2,1,0:T(8,128)} %branches.3, f32[2,256,256]{2,1,0:T(8,128)} %closing.1), custom_call_target="tpu_custom_call" | custom-call | tf_op jit(solution)/shard_map/matrices/pallas_call | solution.py:212
  31.0 92.6 %all-to-all-done = f32[256,32,128]{2,1,0:T(8,128)} async-done(((f32[256,32,128]{2,1,0:T(8,128)}), f32[256,32,128]{2,1,0:T(8,128)}, u32[]{:S(2)}, u32[]{:S(2)}) %all-to-all-start) | async-done | bytes 4194336 | tf_op jit(solution)/shard_map/all_to_all | solution.py:294
  123.6 6.5 %after.1 = f32[2048,128]{1,0:T(8,128)} custom-call(f32[8192,128]{1,0:T(8,128)} %bitcast.1.got, bf16[4,1024,256]{2,1,0:T(8,128)(2,1)S(1)} %get-tuple-element.7.a2, bf16[2,512,512]{2,1,0:T(8,128)(2,1)S(1)} %get-tuple-element.8.c2), custom_call_target="tpu_custom_call" | custom-call | tf_op jit(solution)/shard_map/after/pallas_call | solution.py:212
Async XLA Ops:
  11.2 16.7 %copy-start = (s32[6]{0:T(128)S(1)}, s32[6]{0:T(128)}, u32[]{:S(2)}) copy-start(s32[6]{0:T(128)} %assign.3) | copy-start | bytes 76
  11.2 16.7 %copy-start.1 = (s32[3]{0:T(128)S(1)}, s32[3]{0:T(128)}, u32[]{:S(2)}) copy-start(s32[3]{0:T(128)} %path.3) | copy-start | bytes 40
  11.2 112.4 %all-to-all-start = ((f32[256,32,128]{2,1,0:T(8,128)}), f32[256,32,128]{2,1,0:T(8,128)}, u32[]{:S(2)}, u32[]{:S(2)}) async-start(f32[256,32,128]{2,1,0:T(8,128)} %before.1), calls=%async_computation | async-start | bytes 8388608 | tf_op jit(solution)/shard_map/all_to_all | solution.py:294

commit v5 on v4

--- a/solution.py
+++ b/solution.py
@@ -45,7 +45,7 @@
     return jnp.concatenate(pieces, axis=axis)
 
 
-def before_kernel(assign, path, branches, x, send, words, steps, xs, v, tmp, mix, w1, w0, ys, word_sem, x_sem, v_sem, y_sem):
+def before_kernel(assign, path, branches, x, send, words, steps, xs, v, tmp, w1, w0, ys, word_sem, x_sem, v_sem, y_sem):
     words_in = [pltpu.make_async_copy(a, to, word_sem.at[i]) for i, (a, to) in enumerate(((assign, words), (path, steps)))]
     stem = [
         pltpu.make_async_copy(x.at[p, :, pl.ds(128 * h, 128)], xs.at[p, h], x_sem.at[p, h])
@@ -64,51 +64,49 @@
     for copy in (weights[1], weights[0]):
         copy.start()
 
-    def turn(index, part):
-        turned = v[index, part].T
+    def three(to, re, im):
+        for k, matrix in enumerate((re, im - re, re + im)):
+            to[k, 0], to[k, 1] = halves(matrix)
+
+    def product(x, y, by):
+        k1, k2, k3 = (dot3(stacked(a), (by[k, 0], by[k, 1])) for k, a in enumerate((x + y, x, y)))
+        return k1 - k3, k1 + k2
+
+    weights[1].wait()
+    three(w1, v[1, 0], v[1, 1])
+    weights[0].wait()
+    sorted_parts = []
+    for part in range(2):
+        turned = v[0, part].T
         for h in range(2):
             tmp[h] = turned[:, 128 * h : 128 * h + 128]
-
-    weights[1].wait()
-    for part in range(2):
-        turn(1, part)
-        for h in range(2):
-            for b in range(4):
-                value = tmp[h, pl.ds(b, 64, stride=4), :]
-                mix[h, pl.ds(lax.rem(b + 4 * part + turn_by, 8), 64, stride=8), :] = value
-                mix[2 + h, pl.ds(lax.rem(b + 4 * (1 - part) + turn_by, 8), 64, stride=8), :] = -value if part else value
-    for h in range(4):
-        put(w1, slice(128 * h, 128 * h + 128), slice(0, 512), mix[h].T)
-
+        moved = [cat([tmp[h, pl.ds(b, 64, stride=4), :] for b in range(4)], 0) for h in range(2)]
+        sorted_parts.append(cat(moved, 1).T)
+    three(w0, *sorted_parts)
     for copy in stem:
         copy.wait()
 
     def along_k(m):
-        field = cat([xs[p, h, pl.ds(m, 256, stride=8), :] for p in range(2) for h in range(2)], 1)
-        return dot3(stacked(field), (w1[0], w1[1]))
+        return product(*(cat([xs[p, h, pl.ds(m, 256, stride=8), :] for h in range(2)], 1) for p in range(2)), w1)
 
     def write(m):
-        where = pl.ds(64 * (m // 2), 64), pl.ds(16 * (m % 2), 16)
+        where = pl.ds(32 * (m // 2), 32), slice(None), pl.ds(16 * (m % 2), 16)
         return pltpu.make_async_copy(ys.at[where], send.at[where], y_sem.at[m])
 
     later = [along_k(0), along_k(1)]
-    weights[0].wait()
-    for part in range(2):
-        turn(0, part)
-        moved = [cat([tmp[h, pl.ds(b, 64, stride=4), :] for b in range(4)], 0) for h in range(2)]
-        put(w0, slice(0, 256), slice(256 * part, 256 * part + 256), cat(moved, 1).T)
-    imaginary = lax.rem(lax.broadcasted_iota(jnp.int32, (64, 8, 256), 1) + (8 - turn_by), 8) >= 4
+    upper = lax.broadcasted_iota(jnp.int32, (32, 8, 256), 1) < 4
     for m in range(8):
         c, parity = m // 2, m % 2
         z = later.pop(0)
         if m < 6:
             later.append(along_k(m + 2))
-        u = dot3(stacked(z.T), (w0[0], w0[1])).reshape(64, 8, 512)
-        across = pltpu.roll(u[:, :, 256:], 4, 1)
-        y = u[:, :, :256] + jnp.where(imaginary, across, -across)
-        for bh in range(2):
-            r = 16 * parity + 8 * bh
-            ys[64 * c : 64 * c + 64, r : r + 8, :] = y[:, :, 128 * bh : 128 * bh + 128]
+        re, im = (a.reshape(32, 8, 256) for a in product(z[0].T, z[1].T, w0))
+        crossed = pltpu.roll(jnp.where(upper, im, re), 4, 1)
+        for odd, pair in enumerate((jnp.where(upper, re, crossed), jnp.where(upper, crossed, im))):
+            pair = pltpu.roll(pair, turn_by, 1)
+            for bh in range(2):
+                r = 16 * parity + 8 * bh
+                ys[32 * c : 32 * c + 32, odd, r : r + 8, :] = pair[:, :, 128 * bh : 128 * bh + 128]
         write(m).start()
     for m in range(8):
         write(m).wait()
@@ -229,7 +227,7 @@
         before_kernel,
         [HBM] * 4,
         [HBM],
-        [pltpu.HBM((256, 32, 128), F32)],
+        [pltpu.HBM((128, 2, 32, 128), F32)],
         operands,
         "before",
         [
@@ -238,10 +236,9 @@
             pltpu.VMEM((2, 2, 2048, 128), F32),
             pltpu.VMEM((2, 2, 256, 256), F32),
             pltpu.VMEM((2, 256, 128), F32),
-            pltpu.VMEM((4, 512, 128), F32),
-            pltpu.VMEM((2, 512, 512), BF),
-            pltpu.VMEM((2, 256, 512), BF),
-            pltpu.VMEM((256, 32, 128), F32),
+            pltpu.VMEM((3, 2, 256, 256), BF),
+            pltpu.VMEM((3, 2, 256, 256), BF),
+            pltpu.VMEM((128, 2, 32, 128), F32),
             DMA((2,)),
             DMA((2, 2)),
             DMA((2,)),
@@ -291,7 +288,7 @@
     branches = in_hbm(slice_branches)
     send = before((in_hbm(slice_assign), in_hbm(path), branches, in_hbm(stems.reshape(2, 2048, 256))))
     a2, c2 = matrices((slice_assign, path, branches, in_hbm(closing)))
-    got = lax.all_to_all(send, ALL, 0, 0, tiled=True).reshape(8192, 128)
+    got = lax.all_to_all(send.reshape(256, 32, 128), ALL, 0, 0, tiled=True).reshape(8192, 128)
     out = after(in_hbm(got), a2, c2)
     out = out.reshape(2, 256, 2, 2, 128)
     return jnp.transpose(out, (0, 1, 3, 2, 4)).reshape(2, 256, 2, 256)

time: 130 us -> 130 us (level)
  no operation moved by 1% of the time
where the time goes in v5:
time: 130 us; the launch traced here: 129 us
  waiting for transfers between devices  92.6 us (71%)
  Pallas kernels  19.9 us (15%)
  starting transfers between devices  16.7 us (13%)
    all_to_all x1, waiting for transfers between devices, per_device(): lax.all_to_all(send.reshape(256, 32, 128), ALL, 0, 0, tiled=True)  92.6 us
    pallas_call x3, Pallas kernels, kernel_call(): pl.pallas_call(kernel, in_specs=in_specs, out_specs=out_specs, out_shape=...  19.9 us
    all_to_all x1, starting transfers between devices, per_device(): lax.all_to_all(send.reshape(256, 32, 128), ALL, 0, 0, tiled=True)  16.7 us
  transfers between devices with their start and end apart: 1, of which 1 were waited for; matrix products, arithmetic and copies ran while one was open for 0% of the time, Pallas kernels for 2%

profile of v5, /device:TPU:1, one launch (start us, length us, event | category | flops | bytes accessed | tf_op | source)
XLA Modules:
  0.0 129.4 jit_solution(5618751810891881633)
XLA Ops:
  0.0 10.2 %before.1 = f32[128,2,32,128]{3,2,1,0:T(8,128)} custom-call(s32[6]{0:T(128)} %assign.3, s32[3]{0:T(128)} %path.3, f32[6,3,2,256,256]{4,3,2,1,0:T(8,128)} %branches.3, f32[2,2048,256]{2,1,0:T(8,128)} %bitcast.9), custom_call_target="tpu_custom_call" | custom-call | tf_op jit(solution)/shard_map/before/pallas_call | solution.py:210
  10.2 0.0 copy-start
  10.3 0.0 copy-start.1
  10.3 16.7 %all-to-all-start = ((f32[256,32,128]{2,1,0:T(8,128)}), f32[256,32,128]{2,1,0:T(8,128)}, u32[]{:S(2)}, u32[]{:S(2)}) async-start(f32[256,32,128]{2,1,0:T(8,128)} %bitcast.8), calls=%async_computation | async-start | bytes 8388608 | tf_op jit(solution)/shard_map/all_to_all | solution.py:291
  27.0 0.0 copy-done
  27.0 0.0 copy-done.1
  27.0 3.1 %matrices.1 = (bf16[4,1024,256]{2,1,0:T(8,128)(2,1)S(1)}, bf16[2,512,512]{2,1,0:T(8,128)(2,1)S(1)}) custom-call(s32[6]{0:T(128)S(1)} %copy-done, s32[3]{0:T(128)S(1)} %copy-done.1, f32[6,3,2,256,256]{4,3,2,1,0:T(8,128)} %branches.3, f32[2,256,256]{2,1,0:T(8,128)} %closing.1), custom_call_target="tpu_custom_call" | custom-call | tf_op jit(solution)/shard_map/matrices/pallas_call | solution.py:210
  30.1 92.6 %all-to-all-done = f32[256,32,128]{2,1,0:T(8,128)} async-done(((f32[256,32,128]{2,1,0:T(8,128)}), f32[256,32,128]{2,1,0:T(8,128)}, u32[]{:S(2)}, u32[]{:S(2)}) %all-to-all-start) | async-done | bytes 4194336 | tf_op jit(solution)/shard_map/all_to_all | solution.py:291
  122.7 6.5 %after.1 = f32[2048,128]{1,0:T(8,128)} custom-call(f32[8192,128]{1,0:T(8,128)} %bitcast.2.got, bf16[4,1024,256]{2,1,0:T(8,128)(2,1)S(1)} %get-tuple-element.7.a2, bf16[2,512,512]{2,1,0:T(8,128)(2,1)S(1)} %get-tuple-element.8.c2), custom_call_target="tpu_custom_call" | custom-call | tf_op jit(solution)/shard_map/after/pallas_call | solution.py:210
Async XLA Ops:
  10.2 16.7 %copy-start = (s32[6]{0:T(128)S(1)}, s32[6]{0:T(128)}, u32[]{:S(2)}) copy-start(s32[6]{0:T(128)} %assign.3) | copy-start | bytes 76
  10.3 16.7 %copy-start.1 = (s32[3]{0:T(128)S(1)}, s32[3]{0:T(128)}, u32[]{:S(2)}) copy-start(s32[3]{0:T(128)} %path.3) | copy-start | bytes 40
  10.3 112.4 %all-to-all-start = ((f32[256,32,128]{2,1,0:T(8,128)}), f32[256,32,128]{2,1,0:T(8,128)}, u32[]{:S(2)}, u32[]{:S(2)}) async-start(f32[256,32,128]{2,1,0:T(8,128)} %bitcast.8), calls=%async_computation | async-start | bytes 8388608 | tf_op jit(solution)/shard_map/all_to_all | solution.py:291

commit v6 on v5

--- a/solution.py
+++ b/solution.py
@@ -27,22 +27,18 @@
     return cat(halves(x), 0)
 
 
-def put(pair, rows, cols, value):
-    pair[0, rows, cols], pair[1, rows, cols] = halves(value)
-
-
-def right_blocks(pair, part, value):
-    one, two = slice(0, 256), slice(256, 512)
-    if part == 0:
-        put(pair, one, one, value)
-        put(pair, two, two, value)
-    else:
-        put(pair, one, two, value)
-        put(pair, two, one, -value)
-
-
 def cat(pieces, axis):
     return jnp.concatenate(pieces, axis=axis)
+
+
+def three(to, re, im):
+    for k, matrix in enumerate((re, im - re, re + im)):
+        to[k, 0], to[k, 1] = halves(matrix)
+
+
+def product(x, y, by):
+    k1, k2, k3 = (dot3(stacked(a), (by[k, 0], by[k, 1])) for k, a in enumerate((x + y, x, y)))
+    return k1 - k3, k1 + k2
 
 
 def before_kernel(assign, path, branches, x, send, words, steps, xs, v, tmp, w1, w0, ys, word_sem, x_sem, v_sem, y_sem):
@@ -64,16 +60,19 @@
     for copy in (weights[1], weights[0]):
         copy.start()
 
-    def three(to, re, im):
-        for k, matrix in enumerate((re, im - re, re + im)):
-            to[k, 0], to[k, 1] = halves(matrix)
-
-    def product(x, y, by):
-        k1, k2, k3 = (dot3(stacked(a), (by[k, 0], by[k, 1])) for k, a in enumerate((x + y, x, y)))
-        return k1 - k3, k1 + k2
-
     weights[1].wait()
     three(w1, v[1, 0], v[1, 1])
+    for copy in stem:
+        copy.wait()
+
+    def along_k(m):
+        return product(*(cat([xs[p, h, pl.ds(m, 256, stride=8), :] for h in range(2)], 1) for p in range(2)), w1)
+
+    def write(m):
+        where = pl.ds(32 * (m // 2), 32), slice(None), pl.ds(16 * (m % 2), 16)
+        return pltpu.make_async_copy(ys.at[where], send.at[where], y_sem.at[m])
+
+    later = [along_k(0)]
     weights[0].wait()
     sorted_parts = []
     for part in range(2):
@@ -83,17 +82,7 @@
         moved = [cat([tmp[h, pl.ds(b, 64, stride=4), :] for b in range(4)], 0) for h in range(2)]
         sorted_parts.append(cat(moved, 1).T)
     three(w0, *sorted_parts)
-    for copy in stem:
-        copy.wait()
-
-    def along_k(m):
-        return product(*(cat([xs[p, h, pl.ds(m, 256, stride=8), :] for h in range(2)], 1) for p in range(2)), w1)
-
-    def write(m):
-        where = pl.ds(32 * (m // 2), 32), slice(None), pl.ds(16 * (m % 2), 16)
-        return pltpu.make_async_copy(ys.at[where], send.at[where], y_sem.at[m])
-
-    later = [along_k(0), along_k(1)]
+    later.append(along_k(1))
     upper = lax.broadcasted_iota(jnp.int32, (32, 8, 256), 1) < 4
     for m in range(8):
         c, parity = m // 2, m % 2
@@ -133,11 +122,12 @@
             at = 256 * p
             a2[s, at : at + 256, :], a2[s, 512 + at : 768 + at, :] = halves(cat(moved, 1).T)
     last.wait()
+    parts = []
     for p in range(2):
         for h in range(2):
             tmp[h] = c[p, :, 128 * h : 128 * h + 128]
-        moved = cat([cat([tmp[h, pl.ds(b, 64, stride=4), :] for b in range(4)], 0) for h in range(2)], 1)
-        right_blocks(c2, p, moved)
+        parts.append(cat([cat([tmp[h, pl.ds(b, 64, stride=4), :] for b in range(4)], 0) for h in range(2)], 1))
+    three(c2, *parts)
 
 
 def after_kernel(got, a2, c2, out, rs, os, r_sem, o_sem):
@@ -184,11 +174,9 @@
         terms = [dot3(*pair) for pair in zip(lefts, right, strict=True)]
         total = terms if total is None else [a + b for a, b in zip(total, terms, strict=True)]
     real, imaginary = total[0] - total[1], total[0] + total[2]
-    left = cat([cat([real[:, cols], imaginary[:, cols]], 1) for cols in (slice(0, 256), slice(256, 512))], 0)
-    left = stacked(left)
+    sides = (cat([a[:, :256], a[:, 256:]], 0) for a in (real, imaginary))
     writes = []
-    for q in range(2):
-        result = dot3(left, (c2[0, :, 256 * q : 256 * q + 256], c2[1, :, 256 * q : 256 * q + 256]))
+    for q, result in enumerate(product(*sides, c2)):
         for parity in range(2):
             for h in range(2):
                 value = result[256 * parity : 256 * parity + 256, 128 * h : 128 * h + 128]
@@ -253,7 +241,7 @@
         matrices_kernel,
         [SMEM, SMEM, HBM, HBM],
         [VMEM, VMEM],
-        [shaped(4, 1024, 256, dtype=BF), shaped(2, 512, 512, dtype=BF)],
+        [shaped(4, 1024, 256, dtype=BF), shaped(3, 2, 256, 256, dtype=BF)],
         operands,
         "matrices",
         [

time: 130 us -> 129 us (level)
  no operation moved by 1% of the time
where the time goes in v6:
time: 129 us
  waiting for transfers between devices  92.6 us (72%)
  Pallas kernels  19.6 us (15%)
  starting transfers between devices  16.7 us (13%)
    all_to_all x1, waiting for transfers between devices, per_device(): lax.all_to_all(send.reshape(256, 32, 128), ALL, 0, 0, tiled=True)  92.6 us
    pallas_call x3, Pallas kernels, kernel_call(): pl.pallas_call(kernel, in_specs=in_specs, out_specs=out_specs, out_shape=...  19.6 us
    all_to_all x1, starting transfers between devices, per_device(): lax.all_to_all(send.reshape(256, 32, 128), ALL, 0, 0, tiled=True)  16.7 us
  transfers between devices with their start and end apart: 1, of which 1 were waited for; matrix products, arithmetic and copies ran while one was open for 0% of the time, Pallas kernels for 2%

profile of v6, /device:TPU:1, one launch (start us, length us, event | category | flops | bytes accessed | tf_op | source)
XLA Modules:
  0.0 129.1 jit_solution(825075258496087461)
XLA Ops:
  0.0 10.1 %before.1 = f32[128,2,32,128]{3,2,1,0:T(8,128)} custom-call(s32[6]{0:T(128)} %assign.3, s32[3]{0:T(128)} %path.3, f32[6,3,2,256,256]{4,3,2,1,0:T(8,128)} %branches.3, f32[2,2048,256]{2,1,0:T(8,128)} %bitcast.9), custom_call_target="tpu_custom_call" | custom-call | tf_op jit(solution)/shard_map/before/pallas_call | solution.py:198
  10.1 0.0 copy-start
  10.1 0.0 copy-start.1
  10.1 16.7 %all-to-all-start = ((f32[256,32,128]{2,1,0:T(8,128)}), f32[256,32,128]{2,1,0:T(8,128)}, u32[]{:S(2)}, u32[]{:S(2)}) async-start(f32[256,32,128]{2,1,0:T(8,128)} %bitcast.8), calls=%async_computation | async-start | bytes 8388608 | tf_op jit(solution)/shard_map/all_to_all | solution.py:279
  26.8 0.0 copy-done
  26.8 0.0 copy-done.1
  26.8 3.1 %matrices.1 = (bf16[4,1024,256]{2,1,0:T(8,128)(2,1)S(1)}, bf16[3,2,256,256]{3,2,1,0:T(8,128)(2,1)S(1)}) custom-call(s32[6]{0:T(128)S(1)} %copy-done, s32[3]{0:T(128)S(1)} %copy-done.1, f32[6,3,2,256,256]{4,3,2,1,0:T(8,128)} %branches.3, f32[2,256,256]{2,1,0:T(8,128)} %closing.1), custom_call_target="tpu_custom_call" | custom-call | tf_op jit(solution)/shard_map/matrices/pallas_call | solution.py:198
  30.0 92.6 %all-to-all-done = f32[256,32,128]{2,1,0:T(8,128)} async-done(((f32[256,32,128]{2,1,0:T(8,128)}), f32[256,32,128]{2,1,0:T(8,128)}, u32[]{:S(2)}, u32[]{:S(2)}) %all-to-all-start) | async-done | bytes 4194336 | tf_op jit(solution)/shard_map/all_to_all | solution.py:279
  122.5 6.4 %after.1 = f32[2048,128]{1,0:T(8,128)} custom-call(f32[8192,128]{1,0:T(8,128)} %bitcast.2.got, bf16[4,1024,256]{2,1,0:T(8,128)(2,1)S(1)} %get-tuple-element.7.a2, bf16[3,2,256,256]{3,2,1,0:T(8,128)(2,1)S(1)} %get-tuple-element.8.c2), custom_call_target="tpu_custom_call" | custom-call | tf_op jit(solution)/shard_map/after/pallas_call | solution.py:198
Async XLA Ops:
  10.1 16.7 %copy-start = (s32[6]{0:T(128)S(1)}, s32[6]{0:T(128)}, u32[]{:S(2)}) copy-start(s32[6]{0:T(128)} %assign.3) | copy-start | bytes 76
  10.1 16.7 %copy-start.1 = (s32[3]{0:T(128)S(1)}, s32[3]{0:T(128)}, u32[]{:S(2)}) copy-start(s32[3]{0:T(128)} %path.3) | copy-start | bytes 40
  10.1 112.4 %all-to-all-start = ((f32[256,32,128]{2,1,0:T(8,128)}), f32[256,32,128]{2,1,0:T(8,128)}, u32[]{:S(2)}, u32[]{:S(2)}) async-start(f32[256,32,128]{2,1,0:T(8,128)} %bitcast.8), calls=%async_computation | async-start | bytes 8388608 | tf_op jit(solution)/shard_map/all_to_all | solution.py:279
